TPU v7x, 32 devices: a whole 2x2x4 slice. The times are simulated.
32 devices in a mesh: ep: 2 (over x), kv: 16 (over z, y, core).
Axes of the slice: x: 2, y: 2, z: 4, core: 2. Of those that a mesh axis runs over, the one named last changes fastest.
Arguments:
- queries: bfloat16 [32, 1536], P(('ep', 'kv'))
- key_cache_pages: bfloat16 [512, 64, 512], P(('ep', 'kv'))
- value_cache_pages: bfloat16 [512, 64, 512], P(('ep', 'kv')), may hold values from -5 to 5
- page_table: int32 [32, 65], replicated, may hold values from 0 to 511, as said below
- lengths: int32 [32], replicated, may hold values from 2 to 32768, as said below
- sink_head_logits: float32 [24], replicated, may hold values from -1 to 5
- output_weight: bfloat16 [1536, 1536], replicated, may hold values from -0.15625 to 0.15625
- decode_stream: bfloat16 [32, 1536], P(('ep', 'kv')), may hold values from -6 to 6
- prefill_stream: bfloat16 [4064, 1536], P(('ep', 'kv')), may hold values from -6 to 6
- norm_gain: float32 [1536], replicated, may hold values from 0.1 to 1.9
- expert_gate: bfloat16 [16, 1536, 512], P('kv'), may hold values from -0.15625 to 0.15625
- expert_up: bfloat16 [16, 1536, 512], P('kv'), may hold values from -0.15625 to 0.15625
- expert_down: bfloat16 [16, 512, 1536], P('kv'), may hold values from -0.25 to 0.25
- route_ids: int32 [4096, 8], P(('ep', 'kv')), may hold values from 0 to 15, all different within a row; in each aligned block of 128 rows (0 to 127, 128 to 255, ...) at most 96 rows name the same one
- route_gates: float32 [4096, 8], P(('ep', 'kv')), may hold values from 0.03 to 0.6
Outputs:
- layer_out: bfloat16 [4096, 1536], P(('ep', 'kv'))
Inputs may be any that keep to these rules, and one draw needn't show every extreme that they name: In each aligned block of 16 requests, 1 request, which ones drawn from the seed, have lengths of 4096 or more; the others have lengths of at most 512. `page_table`: no two live slots name the same page. Every slot of a request in aligned block g of 16 requests names a page among g * 16 * 16 to (g + 1) * 16 * 16 - 1. `route_ids`: every row names 8 different experts; among the 128 rows of one device no expert is named by more than 96 rows.
All inputs are finite; a program needn't handle non-finite values.
Results may differ from a plain program's by a relative error of at most 0.0053.
Values may be sent and summed in bfloat16 or wider, within the bound.
A program may use at most 128 MiB of HBM per device.

v0:
```python
import jax
import jax.numpy as jnp
from jax import lax
from jax.sharding import PartitionSpec as P

QUERY_HEADS = 24
KEY_VALUE_HEADS = 8
HEAD_WIDTH = 64
TOPK = 8
WINDOW = 4096
lowest = -1e30


def joined(shard, axis, combine):
    everything = jax.tree.map(lambda part: lax.all_gather(part, axis), shard)
    leading = jax.tree.map(lambda part: part[0], everything)

    def step(k, so_far):
        return combine(so_far, jax.tree.map(lambda part: part[k], everything))

    return lax.fori_loop(1, lax.axis_size(axis), step, leading)


def merge_partials(first_part, second_part):
    max_first, total_first, out_first = first_part
    max_second, total_second, out_second = second_part
    highest = jnp.maximum(max_first, max_second)
    weight_first = jnp.exp(max_first - highest)
    weight_second = jnp.exp(max_second - highest)
    merged_total = total_first * weight_first + total_second * weight_second
    merged_out = out_first * jnp.repeat(weight_first, HEAD_WIDTH, axis=1) + out_second * jnp.repeat(
        weight_second, HEAD_WIDTH, axis=1
    )
    return (highest, merged_total, merged_out)


def rms_rows(stream):
    widened = stream.astype(jnp.float32)
    return widened * lax.rsqrt(jnp.mean(widened * widened, axis=-1, keepdims=True) + 1e-06)


def on_device(
    queries,
    key_cache_pages,
    value_cache_pages,
    page_table,
    lengths,
    sink_head_logits,
    output_weight,
    decode_stream,
    prefill_stream,
    norm_gain,
    expert_gate,
    expert_up,
    expert_down,
    route_ids,
    route_gates,
):
    device_index = lax.axis_index(("ep", "kv"))
    group_index = lax.axis_index("ep")
    member_index = lax.axis_index("kv")
    request_count = lax.axis_size("kv")
    local_pool_index = key_cache_pages.shape[0]
    page_length = key_cache_pages.shape[1]
    win_slots = page_table.shape[1]
    group_width = QUERY_HEADS // KEY_VALUE_HEADS
    score_scale = HEAD_WIDTH ** (-0.5)
    query_rows_full = lax.all_gather(queries, "kv", axis=0, tiled=True)
    group_first = group_index * request_count
    group_table = lax.dynamic_slice_in_dim(page_table, group_first, request_count, 0)
    group_lengths = lax.dynamic_slice_in_dim(lengths, group_first, request_count, 0)
    window_start = jnp.maximum(group_lengths - WINDOW, 0)
    first_page = window_start // page_length
    slot_index = jnp.arange(win_slots, dtype=jnp.int32)
    live_slot = (first_page[:, None] + slot_index[None, :]) * page_length < group_lengths[:, None]
    local_id = group_table - device_index * local_pool_index
    mine = live_slot & (local_id >= 0) & (local_id < local_pool_index)
    target = jnp.where(mine, local_id, local_pool_index).reshape(-1)
    request_grid = jnp.broadcast_to(
        jnp.arange(request_count, dtype=jnp.int32)[:, None], (request_count, win_slots)
    ).reshape(-1)
    slot_grid = jnp.broadcast_to(slot_index[None, :], (request_count, win_slots)).reshape(-1)
    page_request = (
        jnp.full((local_pool_index,), request_count, jnp.int32)
        .at[target]
        .set(request_grid, mode="drop")
    )
    page_slot = jnp.zeros((local_pool_index,), jnp.int32).at[target].set(slot_grid, mode="drop")
    page_used = page_request < request_count
    clamped_request = jnp.minimum(page_request, request_count - 1)
    page_first = (first_page[clamped_request] + page_slot) * page_length
    positions = page_first[:, None] + jnp.arange(page_length, dtype=jnp.int32)[None, :]
    in_window = (
        page_used[:, None]
        & (positions >= window_start[clamped_request][:, None])
        & (positions < group_lengths[clamped_request][:, None])
    )
    queries_of_page = query_rows_full[clamped_request].reshape(
        local_pool_index, KEY_VALUE_HEADS, group_width, HEAD_WIDTH
    )
    key_pieces = key_cache_pages.reshape(local_pool_index, page_length, KEY_VALUE_HEADS, HEAD_WIDTH)
    value_pieces = value_cache_pages.reshape(
        local_pool_index, page_length, KEY_VALUE_HEADS, HEAD_WIDTH
    )
    scores = (
        jnp.einsum(
            "pgqd,ptgd->pgqt", queries_of_page, key_pieces, preferred_element_type=jnp.float32
        )
        * score_scale
    )
    mask_full = in_window[:, None, None, :]
    scores = jnp.where(mask_full, scores, lowest)
    slot_max = jnp.max(scores, axis=-1)
    weights = jnp.where(mask_full, jnp.exp(scores - slot_max[..., None]), 0.0).astype(jnp.bfloat16)
    slot_total = jnp.sum(weights.astype(jnp.float32), axis=-1).reshape(
        local_pool_index, QUERY_HEADS
    )
    slot_out = jnp.einsum(
        "pgqt,ptgd->pgqd", weights, value_pieces, preferred_element_type=jnp.float32
    ).reshape(local_pool_index, QUERY_HEADS, HEAD_WIDTH)
    slot_max = jnp.where(
        page_used[:, None], slot_max.reshape(local_pool_index, QUERY_HEADS), lowest
    )
    owner = (page_request[None, :] == jnp.arange(request_count, dtype=jnp.int32)[:, None])[
        :, :, None
    ]
    request_max = jnp.max(jnp.where(owner, slot_max[None], lowest), axis=1)
    rescale = jnp.where(owner, jnp.exp(slot_max[None] - request_max[:, None]), 0.0)
    request_total = jnp.sum(rescale * slot_total[None], axis=1)
    request_out = jnp.einsum("rph,phd->rhd", rescale, slot_out).reshape(
        request_count, QUERY_HEADS * HEAD_WIDTH
    )
    merged_max, merged_total, merged_out = joined(
        (request_max, request_total, request_out), "kv", merge_partials
    )
    own_max = lax.dynamic_slice_in_dim(merged_max, member_index, 1, 0)
    own_total = lax.dynamic_slice_in_dim(merged_total, member_index, 1, 0)
    own_out = lax.dynamic_slice_in_dim(merged_out, member_index, 1, 0)
    sink_logit_row = sink_head_logits[None, :]
    ceiling = jnp.maximum(own_max, sink_logit_row)
    keep_factor = jnp.exp(own_max - ceiling)
    denominator = own_total * keep_factor + jnp.exp(sink_logit_row - ceiling)
    attended = (own_out * jnp.repeat(keep_factor / denominator, HEAD_WIDTH, axis=1)).astype(
        jnp.bfloat16
    )
    decode_hidden = (
        decode_stream.astype(jnp.float32)
        + jnp.dot(attended, output_weight, preferred_element_type=jnp.float32)
    ).astype(jnp.bfloat16)
    gain_row = norm_gain[None, :]
    normed_prefill = (rms_rows(prefill_stream) * gain_row).astype(jnp.bfloat16)
    normed_decode = (rms_rows(decode_hidden) * gain_row).astype(jnp.bfloat16)
    mixed_rows = jnp.concatenate([prefill_stream, decode_hidden], axis=0)
    residual = mixed_rows.astype(jnp.float32)
    row_count = mixed_rows.shape[0]
    width = mixed_rows.shape[1]
    expert_count = lax.axis_size("kv")
    capacity = min(row_count, 3 * row_count * TOPK // (2 * expert_count))
    pair_expert = route_ids.reshape(-1)
    onehot = (pair_expert[:, None] == jnp.arange(expert_count, dtype=jnp.int32)[None, :]).astype(
        jnp.int32
    )
    pair_rank = jnp.sum((jnp.cumsum(onehot, axis=0) - onehot) * onehot, axis=1)
    pair_slot = pair_expert * capacity + pair_rank
    pair_row = jnp.arange(row_count * TOPK, dtype=jnp.int32) // TOPK
    slot_row = (
        jnp.full((expert_count * capacity,), row_count, jnp.int32).at[pair_slot].set(pair_row)
    )
    normed = jnp.concatenate([normed_prefill, normed_decode], axis=0)
    extended = jnp.concatenate([normed, jnp.zeros((1, width), jnp.bfloat16)], axis=0)
    outgoing = extended[slot_row].reshape(expert_count, capacity, width)
    slot_block = lax.all_to_all(outgoing, "kv", split_axis=0, concat_axis=0, tiled=True)
    gate_part = jnp.einsum(
        "scd,df->scf", slot_block, expert_gate[0], preferred_element_type=jnp.float32
    )
    up_part = jnp.einsum(
        "scd,df->scf", slot_block, expert_up[0], preferred_element_type=jnp.float32
    )
    hidden = (jax.nn.silu(gate_part) * up_part).astype(jnp.bfloat16)
    processed = jnp.einsum(
        "scf,fd->scd", hidden, expert_down[0], preferred_element_type=jnp.float32
    ).astype(jnp.bfloat16)
    returned = lax.all_to_all(processed, "kv", split_axis=0, concat_axis=0, tiled=True).reshape(
        expert_count * capacity, width
    )
    pair_values = returned[pair_slot]
    weighted = (
        pair_values.reshape(row_count, TOPK, width).astype(jnp.float32) * route_gates[:, :, None]
    )
    combined = jnp.sum(weighted, axis=1)
    return (residual + combined).astype(jnp.bfloat16)


def solution(mesh):
    in_specs = (
        P(("ep", "kv"), None),
        P(("ep", "kv"), None, None),
        P(("ep", "kv"), None, None),
        P(),
        P(),
        P(),
        P(),
        P(("ep", "kv"), None),
        P(("ep", "kv"), None),
        P(),
        P("kv", None, None),
        P("kv", None, None),
        P("kv", None, None),
        P(("ep", "kv"), None),
        P(("ep", "kv"), None),
    )
    out_specs = P(("ep", "kv"), None)
    return jax.shard_map(
        on_device, mesh=mesh, in_specs=in_specs, out_specs=out_specs, check_vma=False
    )
```

profile of v0, /device:TPU:13, one launch (start us, length us, event | category | flops | bytes accessed | tf_op | source)
XLA Modules:
  0.0 396.2 jit_solution(12079475339717835462)
XLA Ops:
  6.5 0.9 add_maximum_fusion
  7.4 0.8 fusion.36
  8.4 6.4 %scatter_custom_fusion = s32[16]{0:T(128)S(1)} fusion(s32[1040]{0:T(1024)S(1)} %fusion.43, s32[1040]{0:T(1024)S(1)} %reshape.312, s32[]{:T(128)} %constant.108.clone.1), kind=kCustom, calls=%fused_computation.114 | custom fusion | bytes 68 | tf_op jit(solution)/shard_map/scatter | solution.py:86
  14.9 0.7 gather_fusion
  15.6 0.7 gather_fusion.2
  16.4 6.4 %scatter_custom_fusion.1 = s32[16]{0:T(128)S(1)} fusion(s32[1040]{0:T(1024)S(1)} %fusion.43, s32[1040]{0:T(1024)S(1)} %reshape.320, s32[]{:T(128)} %constant.107.clone.1), kind=kCustom, calls=%fused_computation.111 | custom fusion | bytes 68 | tf_op jit(solution)/shard_map/scatter | solution.py:88
  22.8 0.7 gather_fusion.1
  23.5 16.1 %all-gather.2 = bf16[16,1,1536]{2,1,0:T(2,128)(2,1)S(1)} all-gather(bf16[1,1,1536]{2,1,0:T(2,128)(2,1)} %bitcast.96), channel_id=1, replica_groups=mesh['ep'=2,'kv'=16] {'kv'}, dimensions={0}, use_global_device_ids=true | all-gather | bytes 52224 | tf_op jit(solution)/shard_map/all_gather | solution.py:68
  39.6 0.6 gather_fusion.3
  40.2 0.2 reshape.250
  40.4 2.1 reshape.251
  42.5 3.9 reshape.253
  46.5 2.9 fusion.63
  49.5 2.4 fusion.5
  52.0 0.1 select_reduce_fusion
  52.1 0.2 convolution_bitcast_fusion
  52.4 0.7 all_gather_reshape.3
  53.5 0.4 convert_reduce_fusion
  54.1 0.2 multiply_reduce_fusion
  54.4 21.7 %all-gather.1 = f32[256,24]{1,0:T(8,128)S(1)} all-gather(f32[16,24]{1,0:T(8,128)S(1)} %copy.72), channel_id=3, replica_groups=mesh['ep'=2,'kv'=16] {'kv'}, dimensions={0}, use_global_device_ids=true | all-gather | bytes 26112 | tf_op jit(solution)/shard_map/all_gather | solution.py:15
  76.1 18.0 %all-gather = f32[256,24]{1,0:T(8,128)S(1)} all-gather(f32[16,24]{1,0:T(8,128)S(1)} %copy.70), channel_id=2, replica_groups=mesh['ep'=2,'kv'=16] {'kv'}, dimensions={0}, use_global_device_ids=true | all-gather | bytes 26112 | tf_op jit(solution)/shard_map/all_gather | solution.py:15
  94.1 4.5 %reduce-window.6 = s32[16,8,128]{2,1,0:T(8,128)S(1)} reduce-window(s32[16,8,128]{2,1,0:T(8,128)S(1)} %fusion.31, s32[]{:T(128)} %constant.107.clone.1), window={size=1x1x128 pad=0_0x0_0x127_0}, to_apply=%region_10.11 | reduce-window | flops 2080768 | bytes 131076 | tf_op jit(solution)/shard_map/reduce-window
  98.7 0.1 copy.83
  99.3 4.3 %scatter_custom_fusion.2 = s32[1536]{0:T(1024)S(1)} fusion(s32[1024]{0:T(1024)S(1)} %bitcast.94, s32[1024]{0:T(1024)S(1)} %add_select_fusion, s32[]{:T(128)} %constant.127.clone.1), kind=kCustom, calls=%fused_computation.90 | custom fusion | bytes 6148 | tf_op jit(solution)/shard_map/scatter | solution.py:167
  103.7 0.2 fusion.21
  103.8 0.2 fusion.23
  104.0 0.9 slice_bitcast_fusion
  105.0 21.4 %while.19 = (s32[]{:T(128)}, f32[16,24]{1,0:T(8,128)S(1)}, f32[16,24]{1,0:T(8,128)S(1)}, f32[16,1536]{1,0:T(8,128)S(1)}, f32[16,16,24]{2,1,0:T(8,128)S(1)}, /*in...) while((s32[]{:T(128)}, f32[16,24]{1,0:T(8,128)S(1)}, ...), condition=%wide.region_7.8_spmd, body=%wide.region_6.7_spmd.sunk | while | flops 76037 | bytes 1096855 | solution.py:21
  105.2 0.1 broadcast_in_dim.197
  105.4 0.9 fusion.72
  106.6 0.1 broadcast_in_dim.197
  106.9 0.9 fusion.72
  108.1 0.1 broadcast_in_dim.197
  108.3 0.9 fusion.72
  109.7 0.9 fusion.72
  110.9 0.1 broadcast_in_dim.197
  111.1 0.9 fusion.72
  112.3 0.1 broadcast_in_dim.197
  112.6 0.9 fusion.72
  113.8 0.1 broadcast_in_dim.197
  114.0 0.9 fusion.72
  115.4 0.9 fusion.72
  116.8 0.9 fusion.72
  118.1 0.1 broadcast_in_dim.197
  118.3 0.9 fusion.72
  119.5 0.1 broadcast_in_dim.197
  119.7 0.9 fusion.72
  120.9 0.1 broadcast_in_dim.197
  121.1 0.9 fusion.72
  122.6 0.9 fusion.72
  124.0 0.9 fusion.72
  125.4 0.9 fusion.72
  126.5 3.7 multiply_reduce_fusion.1
  130.9 0.1 maximum_maximum_fusion
  131.1 6.2 %gather_fusion.4 = bf16[1536,1536]{1,0:T(8,128)(2,1)} fusion(bf16[129,1536]{1,0:T(8,128)(2,1)S(1)} %maximum_maximum_fusion, s32[2048]{0:T(1024)S(1)} %pad_clamp_fusion), kind=kCustom, calls=%fused_computation.4 | custom fusion | bytes 9443328 | tf_op jit(solution)/shard_map/gather | solution.py:171
  137.3 111.5 %all_to_all.10 = bf16[16,96,1536]{2,1,0:T(8,128)(2,1)S(1)} all-to-all(bf16[16,96,1536]{2,1,0:T(8,128)(2,1)} %bitcast.86), channel_id=1, replica_groups=mesh['ep'=2,'kv'=16] {'kv'}, dimensions={0} | all-to-all | bytes 9437184 | tf_op jit(solution)/shard_map/all_to_all | solution.py:172
  248.8 2.2 copy-done.1
  251.0 4.2 %fusion.10 = f32[16,96,512]{2,1,0:T(8,128)} fusion(bf16[16,96,1536]{2,1,0:T(8,128)(2,1)S(1)} %all_to_all.10, bf16[1,1536,512]{2,1,0:T(8,128)(2,1)S(1)} %copy-done.9), kind=kOutput, calls=%fused_computation.28 | convolution fusion | flops 2415919104 | bytes 9437184 | tf_op jit(solution)/shard_map/scd,df->scf/dot_general | solution.py:176
  255.2 9.6 %convolution_convert_fusion = bf16[16,96,1536]{2,1,0:T(8,128)(2,1)} fusion(bf16[1,512,1536]{2,1,0:T(8,128)(2,1)S(1)} %copy-done, f32[16,96,512]{2,1,0:T(8,128)} %fusion.10, bf16[16,96,1536]{2,1,0:T(8,128)(2,1)} %copy-done.1, bf16[1,1536,512]{2,1,0:T(8,128)(2,1)} %param.27), kind=kOutput, calls=%fused_computation.19 | convolution fusion | flops 4838916096 | bytes 15728640 | tf_op jit(solution)/shard_map/scf,fd->scd/dot_general | solution.py:180
  264.8 5.0 %all-to-all-start.1 = ((bf16[16,96,1536]{2,1,0:T(8,128)(2,1)}), bf16[16,96,1536]{2,1,0:T(8,128)(2,1)}, u32[]{:S(2)}, u32[]{:S(2)}) async-start(bf16[16,96,1536]{2,1,0:T(8,128)(2,1)} %convolution_convert_fusion), calls=%async_computation.1 | async-start | bytes 9437184 | tf_op jit(solution)/shard_map/all_to_all | solution.py:183
  270.0 103.6 %all-to-all-done.1 = bf16[16,96,1536]{2,1,0:T(8,128)(2,1)} async-done(((bf16[16,96,1536]{2,1,0:T(8,128)(2,1)}), bf16[16,96,1536]{2,1,0:T(8,128)(2,1)}, u32[]{:S(2)}, u32[]{:S(2)}) %all-to-all-start.1) | async-done | bytes 4718624 | tf_op jit(solution)/shard_map/all_to_all | solution.py:183
  373.6 10.2 %gather_fusion.5 = bf16[1024,1536]{1,0:T(8,128)(2,1)} fusion(bf16[1536,1536]{1,0:T(8,128)(2,1)} %bitcast.22, s32[1024]{0:T(1024)S(1)} %broadcast_clamp_fusion), kind=kCustom, calls=%fused_computation.5 | custom fusion | bytes 6295552 | tf_op jit(solution)/shard_map/gather | solution.py:186
  383.8 4.7 %fusion.3 = f32[128,1536]{1,0:T(8,128)S(1)} fusion(bf16[1024,1536]{1,0:T(8,128)(2,1)} %gather_fusion.5, f32[128,8]{1,0:T(8,128)S(1)} %copy.85), kind=kLoop, calls=%fused_computation.18 | loop fusion | flops 4521984 | bytes 3936256 | tf_op jit(solution)/shard_map/reduce_sum | solution.py:190
  388.5 0.8 add_convert_fusion
  (138 shorter events, 7.9 us)
Async XLA Ops:
  6.5 248.7 %copy-start = (bf16[1,512,1536]{2,1,0:T(8,128)(2,1)S(1)}, bf16[1,512,1536]{2,1,0:T(8,128)(2,1)}, u32[]{:S(2)}) copy-start(bf16[1,512,1536]{2,1,0:T(8,128)(2,1)} %param.29) | copy-start | bytes 4718596
  6.5 33.8 %copy-start.3 = (bf16[16,64,512]{2,1,0:T(8,128)(2,1)S(1)}, bf16[16,64,512]{2,1,0:T(8,128)(2,1)}, u32[]{:S(2)}) copy-start(bf16[16,64,512]{2,1,0:T(8,128)(2,1)} %param.18) | copy-start | bytes 3145732
  6.5 97.5 %all-gather.5.cloned.1.call-start = ((), (), s32[]{:S(2)}) async-start(), calls=%async_computation.2 | async-start | bytes 1671168 | tf_op jit(solution)/shard_map/all_gather | solution.py:15
  46.5 6.8 %copy-start.5 = (s32[128,8]{0,1:T(8,128)S(1)}, s32[128,8]{0,1:T(8,128)}, u32[]{:S(2)}) copy-start(s32[128,8]{0,1:T(8,128)} %param.30) | copy-start | bytes 12292
  49.4 54.2 %copy-start.2 = (bf16[127,1536]{1,0:T(8,128)(2,1)S(1)}, bf16[127,1536]{1,0:T(8,128)(2,1)}, u32[]{:S(2)}) copy-start(bf16[127,1536]{1,0:T(8,128)(2,1)} %param.25) | copy-start | bytes 1170436
  49.4 54.4 %copy-start.4 = (f32[1536]{0:T(1024)S(1)}, f32[1536]{0:T(1024)}, u32[]{:S(2)}) copy-start(f32[1536]{0:T(1024)} %param.26) | copy-start | bytes 18436
  104.9 21.4 %copy-start.8 = (f32[24]{0:T(128)S(1)}, f32[24]{0:T(128)}, u32[]{:S(2)}) copy-start(f32[24]{0:T(128)} %param.22) | copy-start | bytes 292
  104.9 21.6 %copy-start.6 = (bf16[1,1536]{1,0:T(2,128)(2,1)S(1)}, bf16[1,1536]{1,0:T(2,128)(2,1)}, u32[]{:S(2)}) copy-start(bf16[1,1536]{1,0:T(2,128)(2,1)} %param.24) | copy-start | bytes 9220
  137.3 113.7 %copy-start.9 = (bf16[1,1536,512]{2,1,0:T(8,128)(2,1)S(1)}, bf16[1,1536,512]{2,1,0:T(8,128)(2,1)}, u32[]{:S(2)}) copy-start(bf16[1,1536,512]{2,1,0:T(8,128)(2,1)} %param.28) | copy-start | bytes 4718596
  248.8 2.2 copy-start.1
  264.8 5.0 %copy-start.7 = (f32[128,8]{0,1:T(8,128)S(1)}, f32[128,8]{0,1:T(8,128)}, u32[]{:S(2)}) copy-start(f32[128,8]{0,1:T(8,128)} %param.31) | copy-start | bytes 12292
  264.8 108.7 %all-to-all-start.1 = ((bf16[16,96,1536]{2,1,0:T(8,128)(2,1)}), bf16[16,96,1536]{2,1,0:T(8,128)(2,1)}, u32[]{:S(2)}, u32[]{:S(2)}) async-start(bf16[16,96,1536]{2,1,0:T(8,128)(2,1)} %convolution_convert_fusion), calls=%async_computation.1 | async-start | bytes 9437184 | tf_op jit(solution)/shard_map/all_to_all | solution.py:183
Sparse Core Ops, SparseCore 0:
  53.3 41.7 all-gather.4
where the time goes:
time: 397 us; the launch traced here: 396 us
  blocking collectives  167 us (42%)
  waiting for transfers between devices  104 us (26%)
  local copies, waits for them, and re-layouts  54.5 us (14%)
  other arithmetic  27.7 us (7%)
  matrix products  22.9 us (6%)
  between operations  14.4 us (4%)
  starting transfers between devices  5.04 us (1%)
    all_to_all x1, blocking collectives, on_device(): lax.all_to_all(outgoing, 'kv', split_axis=0, concat_axis=0, tiled=True)  112 us
    all_to_all x1, waiting for transfers between devices, on_device(): lax.all_to_all(processed, 'kv', split_axis=0, concat_axis=0, tiled=True)  104 us
    all_gather x2, blocking collectives, joined(): everything = jax.tree.map(lambda part: lax.all_gather(part, axis), shard)  39.7 us
    all_gather x1, blocking collectives, on_device(): query_rows_full = lax.all_gather(queries, 'kv', axis=0, tiled=True)  16.1 us
    add x15, other arithmetic, merge_partials(): out_first * jnp.repeat(weight_first, HEAD_WIDTH, axis=1)  14 us
    gather x1, local copies, waits for them, and re-layouts, on_device(): pair_values = returned[pair_slot]  10.2 us
    dot_general x1, matrix products, on_device(): jnp.einsum('scf,fd->scd', hidden, expert_down[0], preferred_element_type=...  9.57 us
  transfers between devices with their start and end apart: 2, of which 1 were waited for; matrix products, arithmetic and copies ran while one was open for 3% of the time, Pallas kernels for 0%

commit v1 on v0

--- a/solution.py
+++ b/solution.py
@@ -9,6 +9,22 @@
 TOPK = 8
 WINDOW = 4096
 lowest = -1e30
+
+
+def ring_gather(x, axis, dim):
+    ways, here, step = (lax.axis_size(axis), lax.axis_index(axis), x.shape[dim])
+    shape = [n * ways if d == dim else n for d, n in enumerate(x.shape)]
+    full = lax.dynamic_update_slice_in_dim(jnp.zeros(shape, x.dtype), x, here * step, axis=dim)
+    going_up = going_down = x
+    for far in range(1, ways // 2 + 1):
+        going_up = lax.ppermute(going_up, axis, [(d, (d + 1) % ways) for d in range(ways)])
+        full = lax.dynamic_update_slice_in_dim(full, going_up, (here - far) % ways * step, axis=dim)
+        if 2 * far < ways:
+            going_down = lax.ppermute(going_down, axis, [(d, (d - 1) % ways) for d in range(ways)])
+            full = lax.dynamic_update_slice_in_dim(
+                full, going_down, (here + far) % ways * step, axis=dim
+            )
+    return full
 
 
 def joined(shard, axis, combine):
@@ -65,7 +81,7 @@
     win_slots = page_table.shape[1]
     group_width = QUERY_HEADS // KEY_VALUE_HEADS
     score_scale = HEAD_WIDTH ** (-0.5)
-    query_rows_full = lax.all_gather(queries, "kv", axis=0, tiled=True)
+    query_rows_full = ring_gather(queries, "kv", 0)
     group_first = group_index * request_count
     group_table = lax.dynamic_slice_in_dim(page_table, group_first, request_count, 0)
     group_lengths = lax.dynamic_slice_in_dim(lengths, group_first, request_count, 0)

time: 397 us -> 415 us (1.045)
  starting transfers between devices: 5.04 us -> 25.6 us
  blocking collectives: 167 us -> 156 us
  waiting for transfers between devices: 104 us -> 110 us
    ppermute x0 -> x15, starting transfers between devices: none -> 20.4 us  [the longest x8 20.3 us: ring_gather(): lax.ppermute(going_up, axis, [(d, (d + 1) % ways) for d in range(ways)])]
    all_gather x1 -> x0, blocking collectives: 16.1 us -> none  [on_device(): query_rows_full = lax.all_gather(queries, 'kv', axis=0, tiled=True)]
    ppermute x0 -> x15, waiting for transfers between devices: none -> 6.46 us  [the longest x7 6.44 us: ring_gather(): lax.ppermute(going_down, axis, [(d, (d - 1) % ways) for d in range(ways)])]
    all_gather x2, blocking collectives: 39.7 us -> 45 us  [joined(): everything = jax.tree.map(lambda part: lax.all_gather(part, axis), shard)]
  transfers between devices with their start and end apart: 2 -> 17, of which waited for: 1 -> 6; matrix products, arithmetic and copies ran while one was open for 3% -> 9% of each run, Pallas kernels for 0% -> 0%
where the time goes in v1:
time: 415 us; the launch traced here: 413 us
  blocking collectives  156 us (38%)
  waiting for transfers between devices  110 us (27%)
  local copies, waits for them, and re-layouts  56 us (13%)
  other arithmetic  27.5 us (7%)
  starting transfers between devices  25.6 us (6%)
  matrix products  22.9 us (6%)
  between operations  14.7 us (4%)
    all_to_all x1, blocking collectives, on_device(): lax.all_to_all(outgoing, 'kv', split_axis=0, concat_axis=0, tiled=True)  111 us
    all_to_all x1, waiting for transfers between devices, on_device(): lax.all_to_all(processed, 'kv', split_axis=0, concat_axis=0, tiled=True)  104 us
    all_gather x2, blocking collectives, joined(): everything = jax.tree.map(lambda part: lax.all_gather(part, axis), shard)  45 us
    ppermute x8, starting transfers between devices, ring_gather(): lax.ppermute(going_up, axis, [(d, (d + 1) % ways) for d in range(ways)])  20.3 us
    add x15, other arithmetic, merge_partials(): out_first * jnp.repeat(weight_first, HEAD_WIDTH, axis=1)  14 us
    gather x1, local copies, waits for them, and re-layouts, on_device(): pair_values = returned[pair_slot]  10.2 us
    dot_general x1, matrix products, on_device(): jnp.einsum('scf,fd->scd', hidden, expert_down[0], preferred_element_type=...  9.56 us
  transfers between devices with their start and end apart: 17, of which 6 were waited for; matrix products, arithmetic and copies ran while one was open for 9% of the time, Pallas kernels for 0%

profile of v1, /device:TPU:13, one launch (start us, length us, event | category | flops | bytes accessed | tf_op | source)
XLA Modules:
  0.0 413.0 jit_solution(2284473237733503840)
XLA Ops:
  6.5 1.8 collective-permute-start
  8.3 0.7 add_maximum_fusion
  9.1 0.8 fusion.36
  10.1 6.4 %scatter_custom_fusion = s32[16]{0:T(128)S(1)} fusion(s32[1040]{0:T(1024)S(1)} %fusion.43, s32[1040]{0:T(1024)S(1)} %reshape.312, s32[]{:T(128)} %constant.188.clone.1), kind=kCustom, calls=%fused_computation.113 | custom fusion | bytes 68 | tf_op jit(solution)/shard_map/scatter | solution.py:102
  16.6 0.7 gather_fusion
  17.3 6.4 %scatter_custom_fusion.1 = s32[16]{0:T(128)S(1)} fusion(s32[1040]{0:T(1024)S(1)} %fusion.43, s32[1040]{0:T(1024)S(1)} %reshape.320, s32[]{:T(128)} %constant.187.clone.1), kind=kCustom, calls=%fused_computation.110 | custom fusion | bytes 68 | tf_op jit(solution)/shard_map/scatter | solution.py:104
  23.8 2.7 collective-permute-start.2
  26.5 0.7 gather_fusion.2
  27.1 0.7 gather_fusion.1
  27.9 2.6 collective-permute-start.4
  30.6 1.2 collective-permute-done.3
  31.8 2.6 collective-permute-start.6
  34.5 1.3 collective-permute-done.5
  35.8 2.6 collective-permute-start.8
  38.4 1.3 collective-permute-done.7
  39.7 2.6 collective-permute-start.10
  42.4 1.3 collective-permute-done.9
  43.7 2.6 collective-permute-start.12
  46.3 1.3 collective-permute-done.11
  47.6 2.6 collective-permute-start.14
  50.3 3.9 reshape.251
  54.2 2.1 reshape.253
  58.0 0.6 gather_fusion.3
  58.6 0.2 reshape.250
  58.8 2.9 fusion.63
  61.8 2.4 fusion.5
  64.4 0.2 convolution_bitcast_fusion
  64.7 0.7 all_gather_reshape.3
  65.8 4.5 %reduce-window.6 = s32[16,8,128]{2,1,0:T(8,128)S(1)} reduce-window(s32[16,8,128]{2,1,0:T(8,128)S(1)} %fusion.31, s32[]{:T(128)} %constant.187.clone.1), window={size=1x1x128 pad=0_0x0_0x127_0}, to_apply=%region_10.11 | reduce-window | flops 2080768 | bytes 131076 | tf_op jit(solution)/shard_map/reduce-window
  71.0 4.3 %scatter_custom_fusion.2 = s32[1536]{0:T(1024)S(1)} fusion(s32[1024]{0:T(1024)S(1)} %bitcast.89, s32[1024]{0:T(1024)S(1)} %add_select_fusion, s32[]{:T(128)} %constant.219.clone.1), kind=kCustom, calls=%fused_computation.89 | custom fusion | bytes 6148 | tf_op jit(solution)/shard_map/scatter | solution.py:183
  75.4 0.2 fusion.21
  75.6 0.2 fusion.23
  75.8 0.4 convert_reduce_fusion
  76.4 0.2 multiply_reduce_fusion
  76.7 26.2 %all-gather.1 = f32[256,24]{1,0:T(8,128)S(1)} all-gather(f32[16,24]{1,0:T(8,128)S(1)} %copy.72), channel_id=3, replica_groups=mesh['ep'=2,'kv'=16] {'kv'}, dimensions={0}, use_global_device_ids=true | all-gather | bytes 26112 | tf_op jit(solution)/shard_map/all_gather | solution.py:31
  102.8 18.8 %all-gather = f32[256,24]{1,0:T(8,128)S(1)} all-gather(f32[16,24]{1,0:T(8,128)S(1)} %copy.70), channel_id=2, replica_groups=mesh['ep'=2,'kv'=16] {'kv'}, dimensions={0}, use_global_device_ids=true | all-gather | bytes 26112 | tf_op jit(solution)/shard_map/all_gather | solution.py:31
  121.7 0.9 slice_bitcast_fusion
  122.6 21.4 %while.19 = (s32[]{:T(128)}, f32[16,24]{1,0:T(8,128)S(1)}, f32[16,24]{1,0:T(8,128)S(1)}, f32[16,1536]{1,0:T(8,128)S(1)}, f32[16,16,24]{2,1,0:T(8,128)S(1)}, /*in...) while((s32[]{:T(128)}, f32[16,24]{1,0:T(8,128)S(1)}, ...), condition=%wide.region_7.8_spmd, body=%wide.region_6.7_spmd.sunk | while | flops 76037 | bytes 1096855 | solution.py:37
  123.1 0.9 fusion.72
  124.5 0.9 fusion.72
  125.9 0.9 fusion.72
  127.3 0.9 fusion.72
  128.8 0.9 fusion.72
  130.2 0.9 fusion.72
  131.6 0.9 fusion.72
  133.0 0.9 fusion.72
  134.5 0.9 fusion.72
  135.9 0.9 fusion.72
  137.3 0.9 fusion.72
  138.7 0.9 fusion.72
  140.2 0.9 fusion.72
  141.6 0.9 fusion.72
  143.0 0.9 fusion.72
  144.2 3.7 multiply_reduce_fusion.1
  148.7 6.2 %gather_fusion.4 = bf16[1536,1536]{1,0:T(8,128)(2,1)} fusion(bf16[129,1536]{1,0:T(8,128)(2,1)S(1)} %maximum_maximum_fusion, s32[2048]{0:T(1024)S(1)} %pad_clamp_fusion), kind=kCustom, calls=%fused_computation.4 | custom fusion | bytes 9443328 | tf_op jit(solution)/shard_map/gather | solution.py:187
  154.9 110.6 %all_to_all.10 = bf16[16,96,1536]{2,1,0:T(8,128)(2,1)S(1)} all-to-all(bf16[16,96,1536]{2,1,0:T(8,128)(2,1)} %bitcast.82), channel_id=1, replica_groups=mesh['ep'=2,'kv'=16] {'kv'}, dimensions={0} | all-to-all | bytes 9437184 | tf_op jit(solution)/shard_map/all_to_all | solution.py:188
  265.5 2.2 copy-done.1
  267.7 4.2 %fusion.10 = f32[16,96,512]{2,1,0:T(8,128)} fusion(bf16[16,96,1536]{2,1,0:T(8,128)(2,1)S(1)} %all_to_all.10, bf16[1,1536,512]{2,1,0:T(8,128)(2,1)S(1)} %copy-done.10), kind=kOutput, calls=%fused_computation.28 | convolution fusion | flops 2415919104 | bytes 9437184 | tf_op jit(solution)/shard_map/scd,df->scf/dot_general | solution.py:192
  271.9 9.6 %convolution_convert_fusion = bf16[16,96,1536]{2,1,0:T(8,128)(2,1)} fusion(bf16[1,512,1536]{2,1,0:T(8,128)(2,1)S(1)} %copy-done, f32[16,96,512]{2,1,0:T(8,128)} %fusion.10, bf16[16,96,1536]{2,1,0:T(8,128)(2,1)} %copy-done.1, bf16[1,1536,512]{2,1,0:T(8,128)(2,1)} %param.27), kind=kOutput, calls=%fused_computation.19 | convolution fusion | flops 4838916096 | bytes 15728640 | tf_op jit(solution)/shard_map/scf,fd->scd/dot_general | solution.py:196
  281.5 5.2 %all-to-all-start.1 = ((bf16[16,96,1536]{2,1,0:T(8,128)(2,1)}), bf16[16,96,1536]{2,1,0:T(8,128)(2,1)}, u32[]{:S(2)}, u32[]{:S(2)}) async-start(bf16[16,96,1536]{2,1,0:T(8,128)(2,1)} %convolution_convert_fusion), calls=%async_computation.1 | async-start | bytes 9437184 | tf_op jit(solution)/shard_map/all_to_all | solution.py:199
  286.8 103.6 %all-to-all-done.1 = bf16[16,96,1536]{2,1,0:T(8,128)(2,1)} async-done(((bf16[16,96,1536]{2,1,0:T(8,128)(2,1)}), bf16[16,96,1536]{2,1,0:T(8,128)(2,1)}, u32[]{:S(2)}, u32[]{:S(2)}) %all-to-all-start.1) | async-done | bytes 4718624 | tf_op jit(solution)/shard_map/all_to_all | solution.py:199
  390.3 10.2 %gather_fusion.5 = bf16[1024,1536]{1,0:T(8,128)(2,1)} fusion(bf16[1536,1536]{1,0:T(8,128)(2,1)} %bitcast.21, s32[1024]{0:T(1024)S(1)} %broadcast_clamp_fusion), kind=kCustom, calls=%fused_computation.5 | custom fusion | bytes 6295552 | tf_op jit(solution)/shard_map/gather | solution.py:202
  400.6 4.7 %fusion.3 = f32[128,1536]{1,0:T(8,128)S(1)} fusion(bf16[1024,1536]{1,0:T(8,128)(2,1)} %gather_fusion.5, f32[128,8]{1,0:T(8,128)S(1)} %copy.85), kind=kLoop, calls=%fused_computation.18 | loop fusion | flops 4521984 | bytes 3936256 | tf_op jit(solution)/shard_map/reduce_sum | solution.py:206
  405.3 0.8 add_convert_fusion
  (185 shorter events, 10.8 us)
Async XLA Ops:
  6.5 265.4 %copy-start = (bf16[1,512,1536]{2,1,0:T(8,128)(2,1)S(1)}, bf16[1,512,1536]{2,1,0:T(8,128)(2,1)}, u32[]{:S(2)}) copy-start(bf16[1,512,1536]{2,1,0:T(8,128)(2,1)} %param.29) | copy-start | bytes 4718596
  6.5 47.7 %copy-start.3 = (bf16[16,64,512]{2,1,0:T(8,128)(2,1)S(1)}, bf16[16,64,512]{2,1,0:T(8,128)(2,1)}, u32[]{:S(2)}) copy-start(bf16[16,64,512]{2,1,0:T(8,128)(2,1)} %param.19) | copy-start | bytes 3145732
  6.5 115.1 %all-gather.4.cloned.1.call-start = ((), (), s32[]{:S(2)}) async-start(), calls=%async_computation.2 | async-start | bytes 1671168 | tf_op jit(solution)/shard_map/all_gather | solution.py:31
  6.5 17.2 %collective-permute-start = (bf16[1,1536]{1,0:T(2,128)(2,1)}, bf16[1,1536]{1,0:T(2,128)(2,1)S(1)}, u32[]{:S(2)}, u32[]{:S(2)}) collective-permute-start(bf16[1,1536]{1,0:T(2,128)(2,1)} %param.17), channel_id=1, source_target_pairs={{0,1},{1,2},{2,3},{3,4},{4,5},{5,6},{6,7},{7,8},{8,9},{9,10},{10,1... | collective-permute-start | bytes 9224 | tf_op jit(solution)/shard_map/ppermute | solution.py:20
  8.3 19.5 %collective-permute-start.1 = (bf16[1,1536]{1,0:T(2,128)(2,1)}, bf16[1,1536]{1,0:T(2,128)(2,1)S(1)}, u32[]{:S(2)}, u32[]{:S(2)}) collective-permute-start(bf16[1,1536]{1,0:T(2,128)(2,1)} %param.17), channel_id=1, source_target_pairs={{0,15},{1,0},{2,1},{3,2},{4,3},{5,4},{6,5},{7,6},{8,7},{9,8},{10,9... | collective-permute-start | bytes 9224 | tf_op jit(solution)/shard_map/ppermute | solution.py:23
  23.8 4.1 collective-permute-start.2
  27.8 4.0 collective-permute-start.3
  27.9 3.9 collective-permute-start.4
  31.8 4.0 collective-permute-start.5
  31.8 4.0 collective-permute-start.6
  35.8 4.0 collective-permute-start.7
  35.8 4.0 collective-permute-start.8
  39.7 4.0 collective-permute-start.9
  39.7 4.0 collective-permute-start.10
  43.7 4.0 collective-permute-start.11
  43.7 4.0 collective-permute-start.12
  47.6 10.2 %collective-permute-start.13 = (bf16[1,1536]{1,0:T(2,128)(2,1)S(1)}, bf16[1,1536]{1,0:T(2,128)(2,1)S(1)}, u32[]{:S(2)}, u32[]{:S(2)}) collective-permute-start(bf16[1,1536]{1,0:T(2,128)(2,1)S(1)} %collective-permute-done.11), channel_id=1, source_target_pairs={{0,15},{1,0},{2,1},{3,2},{4,3},{5,4},{6,5},{7,6},{8,7},{9,8},{10,9... | collective-permute-start | bytes 9224 | tf_op jit(solution)/shard_map/ppermute | solution.py:23
  47.6 10.3 %collective-permute-start.14 = (bf16[1,1536]{1,0:T(2,128)(2,1)S(1)}, bf16[1,1536]{1,0:T(2,128)(2,1)S(1)}, u32[]{:S(2)}, u32[]{:S(2)}) collective-permute-start(bf16[1,1536]{1,0:T(2,128)(2,1)S(1)} %collective-permute-done.12), channel_id=1, source_target_pairs={{0,1},{1,2},{2,3},{3,4},{4,5},{5,6},{6,7},{7,8},{8,9},{9,10},{10,1... | collective-permute-start | bytes 9224 | tf_op jit(solution)/shard_map/ppermute | solution.py:20
  50.3 6.0 %copy-start.6 = (bf16[1,1536]{1,0:T(2,128)(2,1)S(1)}, bf16[1,1536]{1,0:T(2,128)(2,1)}, u32[]{:S(2)}) copy-start(bf16[1,1536]{1,0:T(2,128)(2,1)} %param.17) | copy-start | bytes 9220
  58.8 6.7 %copy-start.5 = (s32[128,8]{0,1:T(8,128)S(1)}, s32[128,8]{0,1:T(8,128)}, u32[]{:S(2)}) copy-start(s32[128,8]{0,1:T(8,128)} %param.30) | copy-start | bytes 12292
  61.7 13.7 %copy-start.2 = (bf16[127,1536]{1,0:T(8,128)(2,1)S(1)}, bf16[127,1536]{1,0:T(8,128)(2,1)}, u32[]{:S(2)}) copy-start(bf16[127,1536]{1,0:T(8,128)(2,1)} %param.25) | copy-start | bytes 1170436
  61.7 13.9 %copy-start.4 = (f32[1536]{0:T(1024)S(1)}, f32[1536]{0:T(1024)}, u32[]{:S(2)}) copy-start(f32[1536]{0:T(1024)} %param.26) | copy-start | bytes 18436
  122.6 21.4 %copy-start.9 = (f32[24]{0:T(128)S(1)}, f32[24]{0:T(128)}, u32[]{:S(2)}) copy-start(f32[24]{0:T(128)} %param.22) | copy-start | bytes 292
  122.6 21.6 %copy-start.7 = (bf16[1,1536]{1,0:T(2,128)(2,1)S(1)}, bf16[1,1536]{1,0:T(2,128)(2,1)}, u32[]{:S(2)}) copy-start(bf16[1,1536]{1,0:T(2,128)(2,1)} %param.24) | copy-start | bytes 9220
  154.9 112.8 %copy-start.10 = (bf16[1,1536,512]{2,1,0:T(8,128)(2,1)S(1)}, bf16[1,1536,512]{2,1,0:T(8,128)(2,1)}, u32[]{:S(2)}) copy-start(bf16[1,1536,512]{2,1,0:T(8,128)(2,1)} %param.28) | copy-start | bytes 4718596
  265.5 2.2 copy-start.1
  281.5 5.2 %copy-start.8 = (f32[128,8]{0,1:T(8,128)S(1)}, f32[128,8]{0,1:T(8,128)}, u32[]{:S(2)}) copy-start(f32[128,8]{0,1:T(8,128)} %param.31) | copy-start | bytes 12292
  281.5 108.9 %all-to-all-start.1 = ((bf16[16,96,1536]{2,1,0:T(8,128)(2,1)}), bf16[16,96,1536]{2,1,0:T(8,128)(2,1)}, u32[]{:S(2)}, u32[]{:S(2)}) async-start(bf16[16,96,1536]{2,1,0:T(8,128)(2,1)} %convolution_convert_fusion), calls=%async_computation.1 | async-start | bytes 9437184 | tf_op jit(solution)/shard_map/all_to_all | solution.py:199
Sparse Core Ops, SparseCore 0:
  65.6 50.4 all-gather.3
